TPU v7x, 256 devices: a whole 4x4x8 slice. The times are simulated.
256 devices in a mesh: dp: 32 (over x_lo, z, core), tensor: 8 (over x_hi, y).
Axes of the slice: x: 4 (x_hi: 2, x_lo: 2; x = x_hi * 2 + x_lo), y: 4, z: 8, core: 2. Of those that a mesh axis runs over, the one named last changes fastest.
Arguments:
- hidden_acts: bfloat16 [256, 256, 14336], P('dp', None, 'tensor'), may hold values from -6 to 6
- out_grads: bfloat16 [256, 256, 4096], P('dp', None, 'tensor'), may hold values from -6 to 6
- input_basis: bfloat16 [64, 14336], P(None, 'tensor'), may hold values from -0.046875 to 0.046875
- output_basis: bfloat16 [64, 4096], P(None, 'tensor'), may hold values from -0.09375 to 0.09375
Outputs:
- gram_block: float32 [256, 256], P('dp', 'tensor')
All inputs are finite; a program needn't handle non-finite values.
Results may differ from a plain program's by a relative error of at most 0.0003.
Values sent between devices are 32-bit elements; how exact they have to be, the bound alone decides.
A program may use at most 64 MiB of HBM per device.

v0:
```python
import math

import jax
import jax.numpy as jnp
from jax import lax
from jax.sharding import PartitionSpec as P


def project(flat, basis):
    return lax.dot_general(
        flat, basis, (((1,), (1,)), ((), ())), preferred_element_type=jnp.float32
    )


def tile_of(feats, other):
    return lax.dot_general(feats, other, (((1,), (1,)), ((), ())), precision=lax.Precision.HIGHEST)


def per_device(hidden_acts, out_grads, input_basis, output_basis):
    seqs, length, width_ff = hidden_acts.shape
    width_k = input_basis.shape[0]
    count_rows = seqs * length
    tensor_count = lax.axis_size("tensor")
    kblock = width_k // tensor_count
    scale = 1.0 / math.sqrt(length * width_k)
    left = project(hidden_acts.reshape(count_rows, width_ff), input_basis)
    right = project(out_grads.reshape(count_rows, out_grads.shape[2]), output_basis)
    left_part = lax.psum_scatter(left, "tensor", scatter_dimension=1, tiled=True)
    right_all = lax.psum(right, "tensor")
    feats = (
        jnp.einsum(
            "sli,slj->sij",
            left_part.reshape(seqs, length, kblock),
            right_all.reshape(seqs, length, width_k),
            precision=lax.Precision.HIGHEST,
        )
        * scale
    )
    feats = feats.reshape(seqs, kblock * width_k)
    tiles = tile_of(feats, lax.all_gather(feats, "dp", axis=0, tiled=True))
    return lax.psum_scatter(tiles, "tensor", scatter_dimension=1, tiled=True)


def solution(mesh):
    return jax.shard_map(
        per_device,
        mesh=mesh,
        in_specs=(
            P("dp", None, "tensor"),
            P("dp", None, "tensor"),
            P(None, "tensor"),
            P(None, "tensor"),
        ),
        out_specs=P("dp", "tensor"),
        check_vma=False,
    )
```

profile of v0, /device:TPU:18, one launch (start us, length us, event | category | flops | bytes accessed | tf_op | source)
XLA Modules:
  0.0 294.6 jit_solution(8691528337902461804)
XLA Ops:
  6.5 0.0 copy-start
  6.5 0.0 all-reduce.2.cloned.1.call-start
  6.5 1.6 copy-done
  8.1 1.6 fusion.1
  9.7 0.8 copy.11
  10.6 0.0 all-reduce.2.cloned.1.call-update
  10.6 0.0 reduce-scatter.5.cloned.1.call-start
  10.6 6.2 %fusion = f32[2048,64]{0,1:T(8,128)} fusion(bf16[2048,1792]{1,0:T(8,128)(2,1)} %bitcast.19, bf16[64,1792]{1,0:T(8,128)(2,1)} %param.6), kind=kOutput, calls=%fused_computation.3 | convolution fusion | flops 469762048 | bytes 8093696 | tf_op jit(solution)/shard_map/dot_general | solution.py:10
  16.8 0.0 reduce-scatter.5.cloned.1.call-update
  16.9 0.0 reduce-scatter.7.cloned.1.call-start
  16.9 83.8 %all-reduce.2.cloned.1.call-done = f32[8,256,64]{1,2,0:T(8,128)} async-done(((f32[8,256,64]{1,2,0:T(8,128)}), f32[8,256,64]{1,2,0:T(8,128)}) %all-reduce.2.cloned.1.call-update) | async-done | bytes 524304 | tf_op jit(solution)/shard_map/psum | solution.py:29
  100.8 78.7 %reduce-scatter.5.cloned.1.call-done = f32[2048,8]{0,1:T(8,128)} async-done(((f32[2048,64]{0,1:T(8,128)}), f32[2048,8]{0,1:T(8,128)}) %reduce-scatter.5.cloned.1.call-update) | async-done | bytes 65552 | tf_op jit(solution)/shard_map/reduce_scatter | solution.py:28
  179.5 1.6 convolution_multiply_fusion
  181.1 0.1 reshape.19
  181.2 35.8 %all_gather.3 = f32[256,512]{1,0:T(8,128)S(1)} all-gather(f32[8,512]{1,0:T(8,128)S(1)} %reshape.19), channel_id=1, replica_groups=mesh['dp'=32,'tensor'=8] {'dp'}, dimensions={0}, use_global_device_ids=true | all-gather | bytes 540672 | tf_op jit(solution)/shard_map/all_gather | solution.py:40
  216.9 1.2 convolution_bitcast_fusion
  218.1 0.0 reduce-scatter.7.cloned.1.call-update
  218.1 68.5 %reduce-scatter.7.cloned.1.call-done = f32[32,8]{1,0:T(8,128)} async-done(((f32[256,8]{1,0:T(8,128)}), f32[32,8]{1,0:T(8,128)}) %reduce-scatter.7.cloned.1.call-update) | async-done | bytes 1040
  286.7 1.4 copy.8
Async XLA Ops:
  6.5 1.6 copy-start
  6.5 94.2 %all-reduce.2.cloned.1.call-start = ((), (), s32[]{:S(2)}) async-start(), calls=%async_computation.3 | async-start | bytes 1048576 | tf_op jit(solution)/shard_map/psum | solution.py:29
  10.6 168.9 %reduce-scatter.5.cloned.1.call-start = ((), (), s32[]{:S(2)}) async-start(), calls=%async_computation.2 | async-start | bytes 589824 | tf_op jit(solution)/shard_map/reduce_scatter | solution.py:28
  16.9 269.8 %reduce-scatter.7.cloned.1.call-start = ((), (), s32[]{:S(2)}) async-start(), calls=%async_computation.4 | async-start | bytes 147456
Sparse Core Ops, SparseCore 0:
  10.7 90.0 all-reduce.1
  105.0 74.4 reduce-scatter.4
  218.3 68.3 reduce-scatter.6
where the time goes:
time: 297 us; the launch traced here: 295 us
  waiting for transfers between devices  231 us (78%)
  blocking collectives  35.8 us (12%)
  between operations  13.1 us (4%)
  matrix products  10.6 us (4%)
  local copies, waits for them, and re-layouts  3.89 us (1%)
    psum x1, waiting for transfers between devices, per_device(): right_all = lax.psum(right, 'tensor')  83.8 us
    reduce_scatter x1, waiting for transfers between devices, per_device(): lax.psum_scatter(left, 'tensor', scatter_dimension=1, tiled=True)  78.7 us
    unnamed x4, waiting for transfers between devices  68.6 us
    all_gather x1, blocking collectives, per_device(): tiles = tile_of(feats, lax.all_gather(feats, 'dp', axis=0, tiled=True))  35.8 us
    dot_general x2, matrix products, project(): lax.dot_general(flat, basis, (((1,), (1,)), ((), ())), preferred_element_...  7.8 us
  transfers between devices with their start and end apart: 3, of which 3 were waited for; matrix products, arithmetic and copies ran while one was open for 2% of the time, Pallas kernels for 0%

commit v1 on v0

v1 whole, which is shorter than its diff:
```python
import math

import jax
import jax.numpy as jnp
from jax import lax
from jax.experimental import pallas as pl
from jax.experimental.pallas import tpu as pltpu
from jax.sharding import PartitionSpec as P

MESH = pl.DeviceIdType.MESH
HIGHEST = lax.Precision.HIGHEST
NT = 8
NQ = 4
NZ = 8


def device(xl, z, c, xh, y):
    return {"dp": xl * 16 + z * 2 + c, "tensor": xh * 4 + y}


def contract_last(a, b, precision=None):
    return lax.dot_general(
        a, b, (((1,), (1,)), ((), ())), precision=precision, preferred_element_type=jnp.float32
    )


def kernel(
    h_hbm, o_hbm, pin_hbm, pout_hbm, out_ref,
    hbuf, obuf, wl, wr, part, recv, fbuf, ebuf, rows, cols, tiles, tiles_in,
    hsem, osem, wsem, rs_send, rs_recv, e_send, e_recv, row_send, row_recv, col_send, col_recv, t_send, t_recv,
):
    dp, me = lax.axis_index("dp"), lax.axis_index("tensor")
    xl, z, c = dp // 16, (dp // 2) % 8, dp % 2
    xh, y = me // 4, me % 4
    q = xl * 2 + c
    zpar, zrow = z % 2, z // 2

    win = pltpu.make_async_copy(pin_hbm, wl.at[pl.ds(0, 64)], wsem.at[0])
    wout = pltpu.make_async_copy(pout_hbm, wr.at[pl.ds(64, 64)], wsem.at[1])
    win.start()
    wout.start()

    def peer(off):
        return lax.rem(xh + off // 4, 2) * 4 + lax.rem(y + off % 4, 4)

    def load(off):
        s = peer(off)
        return (
            pltpu.make_async_copy(h_hbm.at[s], hbuf.at[off], hsem.at[off]),
            pltpu.make_async_copy(o_hbm.at[s], obuf.at[off], osem.at[off]),
        )

    for off in range(NT - 1, -1, -1):
        for copy in load(off):
            copy.start()

    barrier = pltpu.get_barrier_semaphore()

    def greet(dev):
        pl.semaphore_signal(barrier, inc=1, device_id=dev, device_id_type=MESH)

    for off in range(1, NT):
        t = peer(off)
        greet(device(xl, z, c, t // 4, t % 4))
    for j in range(1, NQ):
        p = q ^ j
        greet(device(p // 2, z, p % 2, xh, y))
    for par in range(2):
        src_z = 2 * y + par

        @pl.when(src_z != z)
        def _():
            for t in range(NT):
                greet(device(xl, src_z, c, t // 4, t % 4))

    wl[pl.ds(64, 64), :] = jnp.zeros((64, wl.shape[1]), wl.dtype)
    wr[pl.ds(0, 64), :] = jnp.zeros((64, wr.shape[1]), wr.dtype)
    tiles[...] = jnp.zeros_like(tiles)
    win.wait()
    wout.wait()

    def project(off):
        for copy in load(off):
            copy.wait()
        part[off] = contract_last(hbuf[off], wl[...]) + contract_last(obuf[off], wr[...])

    def rs_copy(off):
        t = peer(off)
        return pltpu.make_async_remote_copy(
            src_ref=part.at[off], dst_ref=recv.at[off], send_sem=rs_send.at[off], recv_sem=rs_recv.at[off],
            device_id=device(xl, z, c, t // 4, t % 4), device_id_type=MESH,
        )

    project(NT - 1)
    pl.semaphore_wait(barrier, (NT - 1) + (NQ - 1) + 2 * (NZ - 1))
    rs_copy(NT - 1).start()

    def step(j, carry):
        off = NT - 1 - j
        project(off)
        rs_copy(off).start()
        return carry

    lax.fori_loop(1, NT - 1, step, 0)
    project(0)

    total = part[0]
    for off in range(NT - 1, 0, -1):
        rs_copy(off).wait_recv()
    for off in range(1, NT):
        total = total + recv[off]

    scale = 1.0 / math.sqrt(256 * 64)
    gram = lax.dot_general(
        total.T[:64], total, (((1,), (0,)), ((), ())), precision=HIGHEST, preferred_element_type=jnp.float32
    ) * scale
    lane = lax.broadcasted_iota(jnp.int32, (32, 128), 1)
    packed = jnp.where(lane < 64, pltpu.roll(gram[:32], 64, 1), gram[32:])
    fbuf[...] = packed.reshape(NQ, 8, 128)

    def e_copy(j):
        p = q ^ j
        return pltpu.make_async_remote_copy(
            src_ref=fbuf.at[p], dst_ref=ebuf.at[q], send_sem=e_send.at[j], recv_sem=e_recv.at[j],
            device_id=device(p // 2, z, p % 2, xh, y), device_id_type=MESH,
        )

    for j in (2, 3, 1):
        e_copy(j).start()
    ebuf[q] = fbuf[q]
    for j in range(1, NQ):
        e_copy(j).wait_recv()

    def col_copy(dz, a):
        return pltpu.make_async_remote_copy(
            src_ref=ebuf.at[pl.ds(2 * a, 2)], dst_ref=cols.at[zpar, me],
            send_sem=col_send, recv_sem=col_recv.at[zpar],
            device_id=device(xl, lax.rem(z + dz, NZ), c, a, zrow), device_id_type=MESH,
        )

    def row_copy(off):
        t = peer(off)
        return pltpu.make_async_remote_copy(
            src_ref=ebuf, dst_ref=rows.at[:, me], send_sem=row_send, recv_sem=row_recv,
            device_id=device(xl, z, c, t // 4, t % 4), device_id_type=MESH,
        )

    for dz in (4, 3, 5, 2, 6, 1, 7):
        for a in range(2):
            col_copy(dz, a).start()
    for off in range(NT - 1, 0, -1):
        row_copy(off).start()
    rows[:, me] = ebuf[...]

    pltpu.make_async_copy(rows.at[:, pl.ds(0, 7)], rows.at[:, pl.ds(0, 7)], row_recv).wait()
    for par in range(2):

        @pl.when(2 * y + par != z)
        def _():
            pltpu.make_async_copy(cols.at[par], cols.at[par], col_recv.at[par]).wait()

        @pl.when(2 * y + par == z)
        def _():
            for cc in range(2):
                cols[par, :, cc] = rows[2 * xh + cc]

    row_all = rows[...].reshape(32, 8, 128)
    acc = jnp.zeros((32, 32), jnp.float32)
    for r in range(8):
        left = row_all[:, r, :]
        right = jnp.concatenate([cols[par, :, cc, r, :] for par in range(2) for cc in range(2)], axis=0)
        acc = acc + contract_last(left, right, HIGHEST)
    tiles[:, :, pl.ds(0, 32)] = acc.reshape(NQ, 8, 32)

    def t_copy(j):
        p = q ^ j
        return pltpu.make_async_remote_copy(
            src_ref=tiles.at[p], dst_ref=tiles_in.at[q], send_sem=t_send.at[j], recv_sem=t_recv.at[j],
            device_id=device(p // 2, z, p % 2, xh, y), device_id_type=MESH,
        )

    for j in (2, 3, 1):
        t_copy(j).start()
    tiles_in[q] = tiles[q]
    for j in range(1, NQ):
        t_copy(j).wait_recv()
    out_ref[...] = (tiles_in[0] + tiles_in[1] + tiles_in[2] + tiles_in[3])[:, :32]

    for off in range(1, NT):
        rs_copy(off).wait_send()
    for j in range(1, NQ):
        e_copy(j).wait_send()
        t_copy(j).wait_send()
    pltpu.make_async_copy(rows.at[:, pl.ds(0, 7)], rows.at[:, pl.ds(0, 7)], row_send).wait()
    pltpu.make_async_copy(rows.at[:, pl.ds(0, 7)], rows.at[:, pl.ds(0, 7)], col_send).wait()


def per_device(hidden_acts, out_grads, input_basis, output_basis):
    seqs, length, width_ff = hidden_acts.shape
    width_d = out_grads.shape[2]
    f32, bf16 = jnp.float32, jnp.bfloat16
    dma, vmem = pltpu.SemaphoreType.DMA, pltpu.VMEM
    return pl.pallas_call(
        kernel,
        out_shape=jax.ShapeDtypeStruct((8, 32), f32),
        in_specs=[pl.BlockSpec(memory_space=pl.ANY)] * 4,
        out_specs=pl.BlockSpec(memory_space=pltpu.VMEM),
        scratch_shapes=[
            vmem((seqs, length, width_ff), bf16),
            vmem((seqs, length, width_d), bf16),
            vmem((128, width_ff), bf16),
            vmem((128, width_d), bf16),
            vmem((NT, length, 128), f32),
            vmem((NT, length, 128), f32),
            vmem((NQ, 8, 128), f32),
            vmem((NQ, 8, 128), f32),
            vmem((NQ, NT, 8, 128), f32),
            vmem((2, NT, 2, 8, 128), f32),
            vmem((NQ, 8, 128), f32),
            vmem((NQ, 8, 128), f32),
            dma((NT,)), dma((NT,)), dma((2,)),
            dma((NT,)), dma((NT,)),
            dma((NQ,)), dma((NQ,)),
            dma, dma,
            dma, dma((2,)),
            dma((NQ,)), dma((NQ,)),
        ],
        compiler_params=pltpu.CompilerParams(
            collective_id=0, has_side_effects=True, vmem_limit_bytes=48 * 2**20
        ),
        cost_estimate=pl.CostEstimate(flops=700_000_000, bytes_accessed=10_000_000, transcendentals=0),
    )(hidden_acts, out_grads, input_basis, output_basis)


def solution(mesh):
    return jax.shard_map(
        per_device,
        mesh=mesh,
        in_specs=(
            P("dp", None, "tensor"),
            P("dp", None, "tensor"),
            P(None, "tensor"),
            P(None, "tensor"),
        ),
        out_specs=P("dp", "tensor"),
        check_vma=False,
    )
```

time: 297 us -> 43.8 us (0.15)
  the two profiles are of different devices: /device:TPU:18 before, /device:TPU:11 now
where the time goes in v1:
time: 43.8 us; the launch traced here: 43.6 us
  Pallas kernels  39.6 us (90%)
  local copies, waits for them, and re-layouts  3.96 us (9%)
    pallas_call x1, Pallas kernels, per_device(): pl.pallas_call(kernel, out_shape=jax.ShapeDtypeStruct((8, 32), f32), in_s...  39.6 us
    unnamed x7, local copies, waits for them, and re-layouts  3.96 us

profile of v1, /device:TPU:11, one launch (start us, length us, event | category | flops | bytes accessed | tf_op | source)
XLA Modules:
  0.0 43.6 jit_solution(12846035805063954531)
XLA Ops:
  0.0 0.0 copy-start
  0.0 1.6 %copy-done = bf16[8,256,512]{2,1,0:T(8,128)(2,1)S(1)} copy-done((bf16[8,256,512]{2,1,0:T(8,128)(2,1)S(1)}, bf16[8,256,512]{2,1,0:T(8,128)(2,1)}, u32[]{:S(2)}) %copy-start) | copy-done | bytes 2097176
  1.6 0.0 copy-start.1
  1.6 0.9 %copy-done.1 = bf16[64,1792]{1,0:T(8,128)(2,1)S(1)} copy-done((bf16[64,1792]{1,0:T(8,128)(2,1)S(1)}, bf16[64,1792]{1,0:T(8,128)(2,1)}, u32[]{:S(2)}) %copy-start.1) | copy-done | bytes 229400
  2.5 0.0 copy-start.2
  2.5 0.8 %copy-done.2 = bf16[64,512]{1,0:T(8,128)(2,1)S(1)} copy-done((bf16[64,512]{1,0:T(8,128)(2,1)S(1)}, bf16[64,512]{1,0:T(8,128)(2,1)}, u32[]{:S(2)}) %copy-start.2) | copy-done | bytes 65560
  3.4 39.6 %shard_map.46 = f32[8,32]{1,0:T(8,128)S(1)} custom-call(bf16[8,256,1792]{2,1,0:T(8,128)(2,1)} %h_hbm.1, bf16[8,256,512]{2,1,0:T(8,128)(2,1)S(1)} %copy-done, bf16[64,1792]{1,0:T(8,128)(2,1)S(1)} %copy-done.1, bf16[64,512]{1,0:T(8,128)(2,1)S(1)} %copy-done.2), custom_call_target="tpu_custom_call" | custom-call | flops 700000000 | bytes 10000000 | tf_op jit(solution)/shard_map/pallas_call | solution.py:203
  43.0 0.6 %copy.6 = f32[8,32]{1,0:T(8,128)} copy(f32[8,32]{1,0:T(8,128)S(1)} %shard_map.46) | data formatting | bytes 2048
Async XLA Ops:
  0.0 1.6 %copy-start = (bf16[8,256,512]{2,1,0:T(8,128)(2,1)S(1)}, bf16[8,256,512]{2,1,0:T(8,128)(2,1)}, u32[]{:S(2)}) copy-start(bf16[8,256,512]{2,1,0:T(8,128)(2,1)} %o_hbm.1) | copy-start | bytes 6291460
  1.6 0.9 %copy-start.1 = (bf16[64,1792]{1,0:T(8,128)(2,1)S(1)}, bf16[64,1792]{1,0:T(8,128)(2,1)}, u32[]{:S(2)}) copy-start(bf16[64,1792]{1,0:T(8,128)(2,1)} %pin_hbm.1) | copy-start | bytes 688132
  2.5 0.8 %copy-start.2 = (bf16[64,512]{1,0:T(8,128)(2,1)S(1)}, bf16[64,512]{1,0:T(8,128)(2,1)}, u32[]{:S(2)}) copy-start(bf16[64,512]{1,0:T(8,128)(2,1)} %pout_hbm.1) | copy-start | bytes 196612

commit v2 on v1

v2 whole, which is shorter than its diff:
```python
import math

import jax
import jax.numpy as jnp
from jax import lax
from jax.experimental import pallas as pl
from jax.experimental.pallas import tpu as pltpu
from jax.sharding import PartitionSpec as P

MESH = pl.DeviceIdType.MESH
HIGHEST = lax.Precision.HIGHEST
NT = 8
NQ = 4
NZ = 8
FROM_X, FROM_YM_O, FROM_YP_O, FROM_YM, FROM_YP, FROM_Y2, FROM_X_SUM = range(7)


def device(xl, z, c, xh, y):
    return {"dp": xl * 16 + z * 2 + c, "tensor": xh * 4 + y}


def contract_last(a, b, precision=None):
    return lax.dot_general(
        a, b, (((1,), (1,)), ((), ())), precision=precision, preferred_element_type=jnp.float32
    )


def kernel(
    h_hbm, o_hbm, pin_hbm, pout_hbm, out_ref,
    hbuf, obuf, wl, wr, part, recv, fbuf, ebuf, rows, cols, tiles, tiles_in,
    hsem, osem, wsem, rs_send, rs_recv, e_send, e_recv, row_send, row_recv, col_send, col_recv, t_send, t_recv,
):
    dp, me = lax.axis_index("dp"), lax.axis_index("tensor")
    xl, z, c = dp // 16, (dp // 2) % 8, dp % 2
    xh, y = me // 4, me % 4
    q = xl * 2 + c
    zpar, zrow = z % 2, z // 2

    def peer(off):
        return lax.rem(xh + off // 4, 2), lax.rem(y + off % 4, 4)

    barrier = pltpu.get_barrier_semaphore()

    def greet(dev):
        pl.semaphore_signal(barrier, inc=1, device_id=dev, device_id_type=MESH)

    for off in range(NT - 1, 0, -1):
        greet(device(xl, z, c, *peer(off)))
    for off in range(NT - 1, -1, -1):
        greet(device(1 - xl, z, c, *peer(off)))
    greet(device(xl, z, 1 - c, xh, y))
    greet(device(1 - xl, z, 1 - c, xh, y))
    for par in range(2):
        src_z = 2 * y + par

        @pl.when(src_z != z)
        def _():
            for t in range(NT):
                greet(device(xh, src_z, c, t // 4, t % 4))

    greetings = 7 + 8 + 2 + 2 * (NZ - 1)

    win = pltpu.make_async_copy(pin_hbm, wl, wsem.at[0])
    wout = pltpu.make_async_copy(pout_hbm, wr, wsem.at[1])

    def load(off):
        a, b = peer(off)
        return (
            pltpu.make_async_copy(h_hbm.at[a * 4 + b], hbuf.at[off], hsem.at[off]),
            pltpu.make_async_copy(o_hbm.at[a * 4 + b], obuf.at[off], osem.at[off]),
        )

    win.start()
    wout.start()
    for off in (6, 5, 7, 4, 1, 3, 2, 0):
        for copy in load(off):
            copy.start()
    tiles[...] = jnp.zeros_like(tiles)
    win.wait()
    wout.wait()

    def project(off):
        for copy in load(off):
            copy.wait()
        part[off, pl.ds(0, 64)] = contract_last(wl[...], hbuf[off])
        part[off, pl.ds(64, 64)] = contract_last(wr[...], obuf[off])

    def rs_copy(off, half, slot, to):
        rowset = pl.ds(64 * half, 64)
        a, b = peer(to)
        return pltpu.make_async_remote_copy(
            src_ref=part.at[off, rowset], dst_ref=recv.at[slot, rowset],
            send_sem=rs_send.at[slot, half], recv_sem=rs_recv.at[slot, half],
            device_id=device(xl, z, c, a, b), device_id_type=MESH,
        )

    x_first = (6, FROM_X, 4)
    o_up, o_down = (5, FROM_YM_O, 1), (7, FROM_YP_O, 3)
    s_up, s_down = (1, FROM_YM, 1), (3, FROM_YP, 3)
    s_across = (2, FROM_Y2, 2)
    x_sum = (4, FROM_X_SUM, 4)

    def start(msg, half):
        rs_copy(msg[0], half, msg[1], msg[2]).start()

    def arrived(msg, half):
        rs_copy(msg[0], half, msg[1], msg[2]).wait_recv()

    for off in (6, 5, 7, 4):
        project(off)
    pl.semaphore_wait(barrier, greetings)
    for half in range(2):
        start(x_first, half)
        start(o_up, half)
        start(o_down, half)
    project(1)
    project(3)
    for half in range(2):
        start(s_up, half)
        start(s_down, half)
    project(2)
    for half in range(2):
        rowset = pl.ds(64 * half, 64)
        arrived(o_up, half)
        arrived(o_down, half)
        part[4, rowset] += recv[FROM_YM_O, rowset] + recv[FROM_YP_O, rowset]
        start(x_sum, half)
        arrived(x_first, half)
        part[2, rowset] += recv[FROM_X, rowset]
        start(s_across, half)
    project(0)
    for msg in (s_up, s_down, x_sum, s_across):
        for half in range(2):
            arrived(msg, half)
    total = (part[0] + recv[FROM_YM]) + (recv[FROM_YP] + recv[FROM_X_SUM]) + recv[FROM_Y2]

    scale = 1.0 / math.sqrt(256 * 64)
    right = total[64:]
    gram = contract_last(total[:64], jnp.concatenate([right, right], axis=0), HIGHEST) * scale
    lane = lax.broadcasted_iota(jnp.int32, (32, 128), 1)
    fbuf[...] = jnp.where(lane < 64, gram[:32], gram[32:]).reshape(2, 2, 8, 128)

    e_copy = pltpu.make_async_remote_copy(
        src_ref=fbuf.at[1 - c], dst_ref=ebuf.at[c], send_sem=e_send, recv_sem=e_recv,
        device_id=device(xl, z, 1 - c, xh, y), device_id_type=MESH,
    )
    e_copy.start()
    ebuf[c] = fbuf[c]
    e_copy.wait_recv()

    def col_copy(dz, to_xl):
        return pltpu.make_async_remote_copy(
            src_ref=ebuf.at[:, to_xl], dst_ref=cols.at[zpar, me],
            send_sem=col_send, recv_sem=col_recv.at[zpar],
            device_id=device(to_xl, lax.rem(z + dz, NZ), c, xl, zrow), device_id_type=MESH,
        )

    def row_copy(off, to_xl):
        return pltpu.make_async_remote_copy(
            src_ref=ebuf.at[:, to_xl], dst_ref=rows.at[pl.ds(2 * xl, 2), me],
            send_sem=row_send, recv_sem=row_recv,
            device_id=device(to_xl, z, c, *peer(off)), device_id_type=MESH,
        )

    for dz in (4, 3, 5, 2, 6, 1, 7):
        for to_xl in (xl, 1 - xl):
            col_copy(dz, to_xl).start()
    for off in range(NT - 1, 0, -1):
        row_copy(off, xl).start()
    for off in range(NT - 1, -1, -1):
        row_copy(off, 1 - xl).start()
    rows[pl.ds(2 * xl, 2), me] = ebuf[:, xl]

    row_bytes = rows.reshape(32, 8, 128).at[pl.ds(0, 30)]
    pltpu.make_async_copy(row_bytes, row_bytes, row_recv).wait()
    for par in range(2):

        @pl.when(2 * y + par != z)
        def _():
            pltpu.make_async_copy(cols.at[par], cols.at[par], col_recv.at[par]).wait()

        @pl.when(2 * y + par == z)
        def _():
            for cc in range(2):
                cols[par, :, cc] = rows[2 * xh + cc]

    row_all = rows[...].reshape(32, 8, 128)
    acc = jnp.zeros((32, 32), jnp.float32)
    for r in range(8):
        col_r = jnp.concatenate([cols[par, :, cc, r, :] for par in range(2) for cc in range(2)], axis=0)
        acc = acc + contract_last(row_all[:, r, :], col_r, HIGHEST)
    tiles[:, :, pl.ds(0, 32)] = acc.reshape(NQ, 8, 32)

    def t_copy(j):
        p = q ^ j
        return pltpu.make_async_remote_copy(
            src_ref=tiles.at[p], dst_ref=tiles_in.at[q], send_sem=t_send.at[j], recv_sem=t_recv.at[j],
            device_id=device(p // 2, z, p % 2, xh, y), device_id_type=MESH,
        )

    for j in (3, 2, 1):
        t_copy(j).start()
    tiles_in[q] = tiles[q]
    for j in range(1, NQ):
        t_copy(j).wait_recv()
    out_ref[...] = (tiles_in[0] + tiles_in[1] + tiles_in[2] + tiles_in[3])[:, :32]

    for msg in (x_first, o_up, o_down, s_up, s_down, s_across, x_sum):
        for half in range(2):
            rs_copy(msg[0], half, msg[1], msg[2]).wait_send()
    e_copy.wait_send()
    for j in range(1, NQ):
        t_copy(j).wait_send()
    pltpu.make_async_copy(row_bytes, row_bytes, row_send).wait()
    col_bytes = rows.reshape(32, 8, 128).at[pl.ds(0, 28)]
    pltpu.make_async_copy(col_bytes, col_bytes, col_send).wait()


def per_device(hidden_acts, out_grads, input_basis, output_basis):
    seqs, length, width_ff = hidden_acts.shape
    width_d = out_grads.shape[2]
    f32, bf16 = jnp.float32, jnp.bfloat16
    dma, vmem = pltpu.SemaphoreType.DMA, pltpu.VMEM
    return pl.pallas_call(
        kernel,
        out_shape=jax.ShapeDtypeStruct((8, 32), f32),
        in_specs=[pl.BlockSpec(memory_space=pltpu.HBM)] * 4,
        out_specs=pl.BlockSpec(memory_space=pltpu.VMEM),
        scratch_shapes=[
            vmem((seqs, length, width_ff), bf16),
            vmem((seqs, length, width_d), bf16),
            vmem((64, width_ff), bf16),
            vmem((64, width_d), bf16),
            vmem((NT, 128, length), f32),
            vmem((7, 128, length), f32),
            vmem((2, 2, 8, 128), f32),
            vmem((2, 2, 8, 128), f32),
            vmem((NQ, NT, 8, 128), f32),
            vmem((2, NT, 2, 8, 128), f32),
            vmem((NQ, 8, 128), f32),
            vmem((NQ, 8, 128), f32),
            dma((NT,)), dma((NT,)), dma((2,)),
            dma((7, 2)), dma((7, 2)),
            dma, dma,
            dma, dma,
            dma, dma((2,)),
            dma((NQ,)), dma((NQ,)),
        ],
        compiler_params=pltpu.CompilerParams(
            collective_id=0, has_side_effects=True, vmem_limit_bytes=62 * 2**20
        ),
        cost_estimate=pl.CostEstimate(flops=700_000_000, bytes_accessed=10_000_000, transcendentals=0),
    )(hidden_acts, out_grads, input_basis, output_basis)


def solution(mesh):
    return jax.shard_map(
        per_device,
        mesh=mesh,
        in_specs=(
            P("dp", None, "tensor"),
            P("dp", None, "tensor"),
            P(None, "tensor"),
            P(None, "tensor"),
        ),
        out_specs=P("dp", "tensor"),
        check_vma=False,
    )
```

time: 43.8 us -> 35.9 us (0.82)
  the two profiles are of different devices: /device:TPU:11 before, /device:TPU:18 now
where the time goes in v2:
time: 35.9 us; the launch traced here: 35.3 us
  Pallas kernels  34 us (95%)
  local copies, waits for them, and re-layouts  1.28 us (4%)
    pallas_call x1, Pallas kernels, per_device(): pl.pallas_call(kernel, out_shape=jax.ShapeDtypeStruct((8, 32), f32), in_s...  34 us
    unnamed x1, local copies, waits for them, and re-layouts  1.28 us

profile of v2, /device:TPU:18, one launch (start us, length us, event | category | flops | bytes accessed | tf_op | source)
XLA Modules:
  0.0 35.3 jit_solution(9583078721908164145)
XLA Ops:
  0.0 34.0 %shard_map.46 = f32[8,32]{1,0:T(8,128)} custom-call(bf16[8,256,1792]{2,1,0:T(8,128)(2,1)} %h_hbm.1, bf16[8,256,512]{2,1,0:T(8,128)(2,1)} %o_hbm.1, bf16[64,1792]{1,0:T(8,128)(2,1)} %pin_hbm.1, bf16[64,512]{1,0:T(8,128)(2,1)} %pout_hbm.1), custom_call_target="tpu_custom_call" | custom-call | flops 700000000 | bytes 10000000 | tf_op jit(solution)/shard_map/pallas_call | solution.py:224
  34.0 1.3 %copy.6 = f32[8,32]{1,0:T(8,128)} copy(f32[8,32]{1,0:T(8,128)} %shard_map.46) | data formatting | bytes 2048

commit v3 on v2

--- a/solution.py
+++ b/solution.py
@@ -12,6 +12,8 @@
 NT = 8
 NQ = 4
 NZ = 8
+ORDER = (6, 5, 7, 4, 1, 3, 2, 0)
+DEPTH = 3
 FROM_X, FROM_YM_O, FROM_YP_O, FROM_YM, FROM_YP, FROM_Y2, FROM_X_SUM = range(7)
 
 
@@ -28,7 +30,7 @@
 def kernel(
     h_hbm, o_hbm, pin_hbm, pout_hbm, out_ref,
     hbuf, obuf, wl, wr, part, recv, fbuf, ebuf, rows, cols, tiles, tiles_in,
-    hsem, osem, wsem, rs_send, rs_recv, e_send, e_recv, row_send, row_recv, col_send, col_recv, t_send, t_recv,
+    hsem, osem, wsem, rs_send, rs_recv, e_send, e_recv, row_send, row_recv, col_send, col_recv, t_send, t_recv, line_sem,
 ):
     dp, me = lax.axis_index("dp"), lax.axis_index("tensor")
     xl, z, c = dp // 16, (dp // 2) % 8, dp % 2
@@ -39,6 +41,22 @@
     def peer(off):
         return lax.rem(xh + off // 4, 2), lax.rem(y + off % 4, 4)
 
+    win = pltpu.make_async_copy(pin_hbm, wl, wsem.at[0])
+    wout = pltpu.make_async_copy(pout_hbm, wr, wsem.at[1])
+
+    def load(off):
+        a, b = peer(off)
+        return (
+            pltpu.make_async_copy(h_hbm.at[a * 4 + b], hbuf.at[off], hsem.at[off]),
+            pltpu.make_async_copy(o_hbm.at[a * 4 + b], obuf.at[off], osem.at[off]),
+        )
+
+    win.start()
+    wout.start()
+    for off in ORDER[:DEPTH]:
+        for copy in load(off):
+            copy.start()
+
     barrier = pltpu.get_barrier_semaphore()
 
     def greet(dev):
@@ -50,31 +68,10 @@
         greet(device(1 - xl, z, c, *peer(off)))
     greet(device(xl, z, 1 - c, xh, y))
     greet(device(1 - xl, z, 1 - c, xh, y))
-    for par in range(2):
-        src_z = 2 * y + par
-
-        @pl.when(src_z != z)
-        def _():
-            for t in range(NT):
-                greet(device(xh, src_z, c, t // 4, t % 4))
-
-    greetings = 7 + 8 + 2 + 2 * (NZ - 1)
-
-    win = pltpu.make_async_copy(pin_hbm, wl, wsem.at[0])
-    wout = pltpu.make_async_copy(pout_hbm, wr, wsem.at[1])
-
-    def load(off):
-        a, b = peer(off)
-        return (
-            pltpu.make_async_copy(h_hbm.at[a * 4 + b], hbuf.at[off], hsem.at[off]),
-            pltpu.make_async_copy(o_hbm.at[a * 4 + b], obuf.at[off], osem.at[off]),
-        )
-
-    win.start()
-    wout.start()
-    for off in (6, 5, 7, 4, 1, 3, 2, 0):
-        for copy in load(off):
-            copy.start()
+    for dz in (4, 3, 5, 2, 6, 1, 7):
+        greet(device(xl, lax.rem(z + dz, NZ), c, xh, y))
+    greetings = 7 + 8 + 2 + 7
+
     tiles[...] = jnp.zeros_like(tiles)
     win.wait()
     wout.wait()
@@ -82,6 +79,10 @@
     def project(off):
         for copy in load(off):
             copy.wait()
+        ahead = ORDER.index(off) + DEPTH
+        if ahead < NT:
+            for copy in load(ORDER[ahead]):
+                copy.start()
         part[off, pl.ds(0, 64)] = contract_last(wl[...], hbuf[off])
         part[off, pl.ds(64, 64)] = contract_last(wr[...], obuf[off])
 
@@ -109,6 +110,17 @@
     for off in (6, 5, 7, 4):
         project(off)
     pl.semaphore_wait(barrier, greetings)
+
+    @pl.when(y == zrow)
+    def _():
+        for t in range(NT):
+
+            @pl.when((xl != xh) | (me != t))
+            def _():
+                pl.semaphore_signal(
+                    line_sem, inc=1, device_id=device(xh, z, c, t // 4, t % 4), device_id_type=MESH
+                )
+
     for half in range(2):
         start(x_first, half)
         start(o_up, half)
@@ -162,6 +174,8 @@
             device_id=device(to_xl, z, c, *peer(off)), device_id_type=MESH,
         )
 
+    own_line = ((xh == xl) & (y == zrow)).astype(jnp.int32)
+    pl.semaphore_wait(line_sem, 2 - own_line)
     for dz in (4, 3, 5, 2, 6, 1, 7):
         for to_xl in (xl, 1 - xl):
             col_copy(dz, to_xl).start()
@@ -245,6 +259,7 @@
             dma, dma,
             dma, dma((2,)),
             dma((NQ,)), dma((NQ,)),
+            pltpu.SemaphoreType.REGULAR,
         ],
         compiler_params=pltpu.CompilerParams(
             collective_id=0, has_side_effects=True, vmem_limit_bytes=62 * 2**20

time: 35.9 us -> 34 us (0.947)
  the two profiles are of different devices: /device:TPU:18 before, /device:TPU:27 now
where the time goes in v3:
time: 34 us; the launch traced here: 33.9 us
  Pallas kernels  32.6 us (96%)
  local copies, waits for them, and re-layouts  1.28 us (4%)
    pallas_call x1, Pallas kernels, per_device(): pl.pallas_call(kernel, out_shape=jax.ShapeDtypeStruct((8, 32), f32), in_s...  32.6 us
    unnamed x1, local copies, waits for them, and re-layouts  1.28 us

profile of v3, /device:TPU:27, one launch (start us, length us, event | category | flops | bytes accessed | tf_op | source)
XLA Modules:
  0.0 33.9 jit_solution(612110303721037634)
XLA Ops:
  0.0 32.6 %shard_map.46 = f32[8,32]{1,0:T(8,128)} custom-call(bf16[8,256,1792]{2,1,0:T(8,128)(2,1)} %h_hbm.1, bf16[8,256,512]{2,1,0:T(8,128)(2,1)} %o_hbm.1, bf16[64,1792]{1,0:T(8,128)(2,1)} %pin_hbm.1, bf16[64,512]{1,0:T(8,128)(2,1)} %pout_hbm.1), custom_call_target="tpu_custom_call" | custom-call | flops 700000000 | bytes 10000000 | tf_op jit(solution)/shard_map/pallas_call | solution.py:238
  32.6 1.3 %copy.6 = f32[8,32]{1,0:T(8,128)} copy(f32[8,32]{1,0:T(8,128)} %shard_map.46) | data formatting | bytes 2048

commit v4 on v2

--- a/solution.py
+++ b/solution.py
@@ -12,6 +12,8 @@
 NT = 8
 NQ = 4
 NZ = 8
+ORDER = (6, 5, 7, 1, 3, 4, 2, 0)
+DEPTH = 3
 FROM_X, FROM_YM_O, FROM_YP_O, FROM_YM, FROM_YP, FROM_Y2, FROM_X_SUM = range(7)
 
 
@@ -28,7 +30,7 @@
 def kernel(
     h_hbm, o_hbm, pin_hbm, pout_hbm, out_ref,
     hbuf, obuf, wl, wr, part, recv, fbuf, ebuf, rows, cols, tiles, tiles_in,
-    hsem, osem, wsem, rs_send, rs_recv, e_send, e_recv, row_send, row_recv, col_send, col_recv, t_send, t_recv,
+    hsem, osem, wsem, rs_send, rs_recv, e_send, e_recv, row_send, row_recv, col_send, col_recv, t_send, t_recv, line_sem, z_sem, xl_sem,
 ):
     dp, me = lax.axis_index("dp"), lax.axis_index("tensor")
     xl, z, c = dp // 16, (dp // 2) % 8, dp % 2
@@ -39,27 +41,6 @@
     def peer(off):
         return lax.rem(xh + off // 4, 2), lax.rem(y + off % 4, 4)
 
-    barrier = pltpu.get_barrier_semaphore()
-
-    def greet(dev):
-        pl.semaphore_signal(barrier, inc=1, device_id=dev, device_id_type=MESH)
-
-    for off in range(NT - 1, 0, -1):
-        greet(device(xl, z, c, *peer(off)))
-    for off in range(NT - 1, -1, -1):
-        greet(device(1 - xl, z, c, *peer(off)))
-    greet(device(xl, z, 1 - c, xh, y))
-    greet(device(1 - xl, z, 1 - c, xh, y))
-    for par in range(2):
-        src_z = 2 * y + par
-
-        @pl.when(src_z != z)
-        def _():
-            for t in range(NT):
-                greet(device(xh, src_z, c, t // 4, t % 4))
-
-    greetings = 7 + 8 + 2 + 2 * (NZ - 1)
-
     win = pltpu.make_async_copy(pin_hbm, wl, wsem.at[0])
     wout = pltpu.make_async_copy(pout_hbm, wr, wsem.at[1])
 
@@ -72,9 +53,22 @@
 
     win.start()
     wout.start()
-    for off in (6, 5, 7, 4, 1, 3, 2, 0):
+    for off in ORDER[:DEPTH]:
         for copy in load(off):
             copy.start()
+
+    barrier = pltpu.get_barrier_semaphore()
+
+    def greet(dev):
+        pl.semaphore_signal(barrier, inc=1, device_id=dev, device_id_type=MESH)
+
+    near = [device(xl, z, c, *peer(off)) for off in (4, 2, 1, 3)]
+    near_z = [device(xl, lax.rem(z + dz, NZ), c, xh, y) for dz in (2, 6, 1, 7)]
+    other_xl = device(1 - xl, z, c, xh, y)
+    for dev in near + [device(1 - xl, z, 1 - c, xh, y)] + near_z + [other_xl, device(xl, z, 1 - c, xh, y)]:
+        greet(dev)
+    greetings = 11
+
     tiles[...] = jnp.zeros_like(tiles)
     win.wait()
     wout.wait()
@@ -82,6 +76,10 @@
     def project(off):
         for copy in load(off):
             copy.wait()
+        ahead = ORDER.index(off) + DEPTH
+        if ahead < NT:
+            for copy in load(ORDER[ahead]):
+                copy.start()
         part[off, pl.ds(0, 64)] = contract_last(wl[...], hbuf[off])
         part[off, pl.ds(64, 64)] = contract_last(wr[...], obuf[off])
 
@@ -106,18 +104,21 @@
     def arrived(msg, half):
         rs_copy(msg[0], half, msg[1], msg[2]).wait_recv()
 
-    for off in (6, 5, 7, 4):
+    for off in (6, 5, 7):
         project(off)
     pl.semaphore_wait(barrier, greetings)
     for half in range(2):
         start(x_first, half)
         start(o_up, half)
         start(o_down, half)
+    for dev in near_z:
+        pl.semaphore_signal(z_sem, inc=1, device_id=dev, device_id_type=MESH)
     project(1)
     project(3)
     for half in range(2):
         start(s_up, half)
         start(s_down, half)
+    project(4)
     project(2)
     for half in range(2):
         rowset = pl.ds(64 * half, 64)
@@ -128,6 +129,21 @@
         arrived(x_first, half)
         part[2, rowset] += recv[FROM_X, rowset]
         start(s_across, half)
+        if half == 0:
+            pl.semaphore_signal(xl_sem, inc=1, device_id=other_xl, device_id_type=MESH)
+
+    pl.semaphore_wait(z_sem, 4)
+    pl.semaphore_wait(xl_sem, 1)
+
+    @pl.when(y == zrow)
+    def _():
+        for t in range(NT):
+
+            @pl.when((xl != xh) | (me != t))
+            def _():
+                pl.semaphore_signal(
+                    line_sem, inc=1, device_id=device(xh, z, c, t // 4, t % 4), device_id_type=MESH
+                )
     project(0)
     for msg in (s_up, s_down, x_sum, s_across):
         for half in range(2):
@@ -162,6 +178,8 @@
             device_id=device(to_xl, z, c, *peer(off)), device_id_type=MESH,
         )
 
+    own_line = ((xh == xl) & (y == zrow)).astype(jnp.int32)
+    pl.semaphore_wait(line_sem, 2 - own_line)
     for dz in (4, 3, 5, 2, 6, 1, 7):
         for to_xl in (xl, 1 - xl):
             col_copy(dz, to_xl).start()
@@ -245,9 +263,10 @@
             dma, dma,
             dma, dma((2,)),
             dma((NQ,)), dma((NQ,)),
+            pltpu.SemaphoreType.REGULAR, pltpu.SemaphoreType.REGULAR, pltpu.SemaphoreType.REGULAR,
         ],
         compiler_params=pltpu.CompilerParams(
-            collective_id=0, has_side_effects=True, vmem_limit_bytes=62 * 2**20
+            collective_id=0, has_side_effects=True, vmem_limit_bytes=55168 * 1024
         ),
         cost_estimate=pl.CostEstimate(flops=700_000_000, bytes_accessed=10_000_000, transcendentals=0),
     )(hidden_acts, out_grads, input_basis, output_basis)

time: 35.9 us -> 31.9 us (0.89)
  Pallas kernels: 34 us -> 30.8 us
  local copies, waits for them, and re-layouts: 1.28 us -> 0.6 us
    pallas_call x1, Pallas kernels: 34 us -> 30.8 us  [per_device(): pl.pallas_call(kernel, out_shape=jax.ShapeDtypeStruct((8, 32), f32), in_s...]
    unnamed x1, local copies, waits for them, and re-layouts: 1.28 us -> 0.6 us
where the time goes in v4:
time: 31.9 us; the launch traced here: 31.4 us
  Pallas kernels  30.8 us (97%)
  local copies, waits for them, and re-layouts  0.6 us (2%)
    pallas_call x1, Pallas kernels, per_device(): pl.pallas_call(kernel, out_shape=jax.ShapeDtypeStruct((8, 32), f32), in_s...  30.8 us

profile of v4, /device:TPU:18, one launch (start us, length us, event | category | flops | bytes accessed | tf_op | source)
XLA Modules:
  0.0 31.4 jit_solution(4712960159485256376)
XLA Ops:
  0.0 30.8 %shard_map.46 = f32[8,32]{1,0:T(8,128)S(1)} custom-call(bf16[8,256,1792]{2,1,0:T(8,128)(2,1)} %h_hbm.1, bf16[8,256,512]{2,1,0:T(8,128)(2,1)} %o_hbm.1, bf16[64,1792]{1,0:T(8,128)(2,1)} %pin_hbm.1, bf16[64,512]{1,0:T(8,128)(2,1)} %pout_hbm.1), custom_call_target="tpu_custom_call" | custom-call | flops 700000000 | bytes 10000000 | tf_op jit(solution)/shard_map/pallas_call | solution.py:242
  30.8 0.6 %copy.6 = f32[8,32]{1,0:T(8,128)} copy(f32[8,32]{1,0:T(8,128)S(1)} %shard_map.46) | data formatting | bytes 2048

commit v5 on v4

--- a/solution.py
+++ b/solution.py
@@ -12,9 +12,19 @@
 NT = 8
 NQ = 4
 NZ = 8
-ORDER = (6, 5, 7, 1, 3, 4, 2, 0)
+ORDER = (5, 7, 6, 1, 3, 4, 2, 0)
 DEPTH = 3
 FROM_X, FROM_YM_O, FROM_YP_O, FROM_YM, FROM_YP, FROM_Y2, FROM_X_SUM = range(7)
+CUT = 112
+X_FIRST = ((6, 0, 64, FROM_X, 4), (6, 64, 64, FROM_X, 4))
+X_UP, X_DOWN = (5, CUT, 128 - CUT, FROM_YM_O, 4), (7, CUT, 128 - CUT, FROM_YP_O, 4)
+O_UP = tuple((5, r, CUT // 2, FROM_YM_O, 1) for r in (0, CUT // 2))
+O_DOWN = tuple((7, r, CUT // 2, FROM_YP_O, 3) for r in (0, CUT // 2))
+S_UP = ((1, 0, CUT, FROM_YM, 1), (1, CUT, 128 - CUT, FROM_YM, 1))
+S_DOWN = ((3, 0, CUT, FROM_YP, 3), (3, CUT, 128 - CUT, FROM_YP, 3))
+S_ACROSS = ((2, 0, 64, FROM_Y2, 2), (2, 64, 64, FROM_Y2, 2))
+X_SUM = ((4, 0, CUT // 2, FROM_X_SUM, 4), (4, CUT // 2, CUT // 2, FROM_X_SUM, 4), (4, CUT, 128 - CUT, FROM_X_SUM, 4))
+MESSAGES = X_FIRST + (X_UP, X_DOWN) + O_UP + O_DOWN + S_UP + S_DOWN + S_ACROSS + X_SUM
 
 
 def device(xl, z, c, xh, y):
@@ -83,54 +93,52 @@
         part[off, pl.ds(0, 64)] = contract_last(wl[...], hbuf[off])
         part[off, pl.ds(64, 64)] = contract_last(wr[...], obuf[off])
 
-    def rs_copy(off, half, slot, to):
-        rowset = pl.ds(64 * half, 64)
-        a, b = peer(to)
-        return pltpu.make_async_remote_copy(
-            src_ref=part.at[off, rowset], dst_ref=recv.at[slot, rowset],
-            send_sem=rs_send.at[slot, half], recv_sem=rs_recv.at[slot, half],
-            device_id=device(xl, z, c, a, b), device_id_type=MESH,
-        )
-
-    x_first = (6, FROM_X, 4)
-    o_up, o_down = (5, FROM_YM_O, 1), (7, FROM_YP_O, 3)
-    s_up, s_down = (1, FROM_YM, 1), (3, FROM_YP, 3)
-    s_across = (2, FROM_Y2, 2)
-    x_sum = (4, FROM_X_SUM, 4)
-
-    def start(msg, half):
-        rs_copy(msg[0], half, msg[1], msg[2]).start()
-
-    def arrived(msg, half):
-        rs_copy(msg[0], half, msg[1], msg[2]).wait_recv()
-
-    for off in (6, 5, 7):
+    def rs_copy(msg):
+        chunk, row, count, slot, to = msg
+        at = MESSAGES.index(msg)
+        return pltpu.make_async_remote_copy(
+            src_ref=part.at[chunk, pl.ds(row, count)], dst_ref=recv.at[slot, pl.ds(row, count)],
+            send_sem=rs_send.at[at], recv_sem=rs_recv.at[at],
+            device_id=device(xl, z, c, *peer(to)), device_id_type=MESH,
+        )
+
+    def start(*messages):
+        for msg in messages:
+            rs_copy(msg).start()
+
+    def arrived(*messages):
+        for msg in messages:
+            rs_copy(msg).wait_recv()
+
+    for off in (5, 7, 6):
         project(off)
     pl.semaphore_wait(barrier, greetings)
-    for half in range(2):
-        start(x_first, half)
-        start(o_up, half)
-        start(o_down, half)
+    start(O_UP[0], O_DOWN[0], X_FIRST[0], O_UP[1], O_DOWN[1], X_FIRST[1], X_UP, X_DOWN)
     for dev in near_z:
         pl.semaphore_signal(z_sem, inc=1, device_id=dev, device_id_type=MESH)
     project(1)
+    start(S_UP[0])
     project(3)
-    for half in range(2):
-        start(s_up, half)
-        start(s_down, half)
+    start(S_DOWN[0])
     project(4)
+    start(X_SUM[2])
     project(2)
     for half in range(2):
+        arrived(O_UP[half], O_DOWN[half])
+        rowset = pl.ds(CUT // 2 * half, CUT // 2)
+        part[4, rowset] += recv[FROM_YM_O, rowset] + recv[FROM_YP_O, rowset]
+        start(X_SUM[half])
+        arrived(X_FIRST[half])
         rowset = pl.ds(64 * half, 64)
-        arrived(o_up, half)
-        arrived(o_down, half)
-        part[4, rowset] += recv[FROM_YM_O, rowset] + recv[FROM_YP_O, rowset]
-        start(x_sum, half)
-        arrived(x_first, half)
         part[2, rowset] += recv[FROM_X, rowset]
-        start(s_across, half)
+        start(S_ACROSS[half])
         if half == 0:
             pl.semaphore_signal(xl_sem, inc=1, device_id=other_xl, device_id_type=MESH)
+    arrived(X_UP, X_DOWN)
+    rowset = pl.ds(CUT, 128 - CUT)
+    part[1, rowset] += recv[FROM_YM_O, rowset]
+    part[3, rowset] += recv[FROM_YP_O, rowset]
+    start(S_UP[1], S_DOWN[1])
 
     pl.semaphore_wait(z_sem, 4)
     pl.semaphore_wait(xl_sem, 1)
@@ -145,9 +153,7 @@
                     line_sem, inc=1, device_id=device(xh, z, c, t // 4, t % 4), device_id_type=MESH
                 )
     project(0)
-    for msg in (s_up, s_down, x_sum, s_across):
-        for half in range(2):
-            arrived(msg, half)
+    arrived(*S_UP, *S_DOWN, *X_SUM, *S_ACROSS)
     total = (part[0] + recv[FROM_YM]) + (recv[FROM_YP] + recv[FROM_X_SUM]) + recv[FROM_Y2]
 
     scale = 1.0 / math.sqrt(256 * 64)
@@ -157,37 +163,38 @@
     fbuf[...] = jnp.where(lane < 64, gram[:32], gram[32:]).reshape(2, 2, 8, 128)
 
     e_copy = pltpu.make_async_remote_copy(
-        src_ref=fbuf.at[1 - c], dst_ref=ebuf.at[c], send_sem=e_send, recv_sem=e_recv,
+        src_ref=fbuf.at[1 - c], dst_ref=ebuf.at[:, c], send_sem=e_send, recv_sem=e_recv,
         device_id=device(xl, z, 1 - c, xh, y), device_id_type=MESH,
     )
     e_copy.start()
-    ebuf[c] = fbuf[c]
+    ebuf[:, c] = fbuf[c]
     e_copy.wait_recv()
 
-    def col_copy(dz, to_xl):
-        return pltpu.make_async_remote_copy(
-            src_ref=ebuf.at[:, to_xl], dst_ref=cols.at[zpar, me],
+    def col_copy(to_z, to_xl):
+        return pltpu.make_async_remote_copy(
+            src_ref=ebuf.at[to_xl], dst_ref=cols.at[zpar, me],
             send_sem=col_send, recv_sem=col_recv.at[zpar],
-            device_id=device(to_xl, lax.rem(z + dz, NZ), c, xl, zrow), device_id_type=MESH,
+            device_id=device(to_xl, to_z, c, xl, zrow), device_id_type=MESH,
         )
 
     def row_copy(off, to_xl):
         return pltpu.make_async_remote_copy(
-            src_ref=ebuf.at[:, to_xl], dst_ref=rows.at[pl.ds(2 * xl, 2), me],
+            src_ref=ebuf.at[to_xl], dst_ref=rows.at[xl, me],
             send_sem=row_send, recv_sem=row_recv,
             device_id=device(to_xl, z, c, *peer(off)), device_id_type=MESH,
         )
 
     own_line = ((xh == xl) & (y == zrow)).astype(jnp.int32)
     pl.semaphore_wait(line_sem, 2 - own_line)
-    for dz in (4, 3, 5, 2, 6, 1, 7):
-        for to_xl in (xl, 1 - xl):
-            col_copy(dz, to_xl).start()
+    for i in range(NZ - 1):
+        to_z = jnp.where(i < z, i, i + 1)
+        for to_xl in (1 - xl, xl):
+            col_copy(to_z, to_xl).start()
     for off in range(NT - 1, 0, -1):
         row_copy(off, xl).start()
     for off in range(NT - 1, -1, -1):
         row_copy(off, 1 - xl).start()
-    rows[pl.ds(2 * xl, 2), me] = ebuf[:, xl]
+    rows[xl, me] = ebuf[xl]
 
     row_bytes = rows.reshape(32, 8, 128).at[pl.ds(0, 30)]
     pltpu.make_async_copy(row_bytes, row_bytes, row_recv).wait()
@@ -199,14 +206,13 @@
 
         @pl.when(2 * y + par == z)
         def _():
-            for cc in range(2):
-                cols[par, :, cc] = rows[2 * xh + cc]
-
-    row_all = rows[...].reshape(32, 8, 128)
+            cols[par] = rows[xh]
+
     acc = jnp.zeros((32, 32), jnp.float32)
     for r in range(8):
         col_r = jnp.concatenate([cols[par, :, cc, r, :] for par in range(2) for cc in range(2)], axis=0)
-        acc = acc + contract_last(row_all[:, r, :], col_r, HIGHEST)
+        row_r = jnp.concatenate([rows[a, :, cc, r, :] for a in range(2) for cc in range(2)], axis=0)
+        acc = acc + contract_last(row_r, col_r, HIGHEST)
     tiles[:, :, pl.ds(0, 32)] = acc.reshape(NQ, 8, 32)
 
     def t_copy(j):
@@ -223,9 +229,8 @@
         t_copy(j).wait_recv()
     out_ref[...] = (tiles_in[0] + tiles_in[1] + tiles_in[2] + tiles_in[3])[:, :32]
 
-    for msg in (x_first, o_up, o_down, s_up, s_down, s_across, x_sum):
-        for half in range(2):
-            rs_copy(msg[0], half, msg[1], msg[2]).wait_send()
+    for msg in MESSAGES:
+        rs_copy(msg).wait_send()
     e_copy.wait_send()
     for j in range(1, NQ):
         t_copy(j).wait_send()
@@ -253,12 +258,12 @@
             vmem((7, 128, length), f32),
             vmem((2, 2, 8, 128), f32),
             vmem((2, 2, 8, 128), f32),
-            vmem((NQ, NT, 8, 128), f32),
+            vmem((2, NT, 2, 8, 128), f32),
             vmem((2, NT, 2, 8, 128), f32),
             vmem((NQ, 8, 128), f32),
             vmem((NQ, 8, 128), f32),
             dma((NT,)), dma((NT,)), dma((2,)),
-            dma((7, 2)), dma((7, 2)),
+            dma((len(MESSAGES),)), dma((len(MESSAGES),)),
             dma, dma,
             dma, dma,
             dma, dma((2,)),

time: 31.9 us -> 31.1 us (0.975)
  Pallas kernels: 30.8 us -> 30.3 us
    pallas_call x1, Pallas kernels: 30.8 us -> 30.3 us  [per_device(): pl.pallas_call(kernel, out_shape=jax.ShapeDtypeStruct((8, 32), f32), in_s...]
where the time goes in v5:
time: 31.1 us; the launch traced here: 30.9 us
  Pallas kernels  30.3 us (97%)
  local copies, waits for them, and re-layouts  0.6 us (2%)
    pallas_call x1, Pallas kernels, per_device(): pl.pallas_call(kernel, out_shape=jax.ShapeDtypeStruct((8, 32), f32), in_s...  30.3 us

profile of v5, /device:TPU:18, one launch (start us, length us, event | category | flops | bytes accessed | tf_op | source)
XLA Modules:
  0.0 30.9 jit_solution(17131231650427458969)
XLA Ops:
  0.0 30.3 %shard_map.46 = f32[8,32]{1,0:T(8,128)S(1)} custom-call(bf16[8,256,1792]{2,1,0:T(8,128)(2,1)} %h_hbm.1, bf16[8,256,512]{2,1,0:T(8,128)(2,1)} %o_hbm.1, bf16[64,1792]{1,0:T(8,128)(2,1)} %pin_hbm.1, bf16[64,512]{1,0:T(8,128)(2,1)} %pout_hbm.1), custom_call_target="tpu_custom_call" | custom-call | flops 700000000 | bytes 10000000 | tf_op jit(solution)/shard_map/pallas_call | solution.py:247
  30.3 0.6 %copy.6 = f32[8,32]{1,0:T(8,128)} copy(f32[8,32]{1,0:T(8,128)S(1)} %shard_map.46) | data formatting | bytes 2048

commit v6 on v5

--- a/solution.py
+++ b/solution.py
@@ -37,10 +37,15 @@
     )
 
 
+def split(x):
+    high = x.astype(jnp.bfloat16)
+    return high, (x - high.astype(jnp.float32)).astype(jnp.bfloat16)
+
+
 def kernel(
     h_hbm, o_hbm, pin_hbm, pout_hbm, out_ref,
-    hbuf, obuf, wl, wr, part, recv, fbuf, ebuf, rows, cols, tiles, tiles_in,
-    hsem, osem, wsem, rs_send, rs_recv, e_send, e_recv, row_send, row_recv, col_send, col_recv, t_send, t_recv, line_sem, z_sem, xl_sem,
+    hbuf, obuf, wl, wr, part, recv, fbuf, rows, cols, tiles, tiles_in,
+    hsem, osem, wsem, rs_send, rs_recv, row_send, row_recv, col_send, col_recv, t_send, t_recv, line_sem, z_sem, plane_sem,
 ):
     dp, me = lax.axis_index("dp"), lax.axis_index("tensor")
     xl, z, c = dp // 16, (dp // 2) % 8, dp % 2
@@ -74,8 +79,8 @@
 
     near = [device(xl, z, c, *peer(off)) for off in (4, 2, 1, 3)]
     near_z = [device(xl, lax.rem(z + dz, NZ), c, xh, y) for dz in (2, 6, 1, 7)]
-    other_xl = device(1 - xl, z, c, xh, y)
-    for dev in near + [device(1 - xl, z, 1 - c, xh, y)] + near_z + [other_xl, device(xl, z, 1 - c, xh, y)]:
+    others = [device(1 - xl, z, 1 - c, xh, y), device(1 - xl, z, c, xh, y), device(xl, z, 1 - c, xh, y)]
+    for dev in near + near_z + others:
         greet(dev)
     greetings = 11
 
@@ -133,7 +138,8 @@
         part[2, rowset] += recv[FROM_X, rowset]
         start(S_ACROSS[half])
         if half == 0:
-            pl.semaphore_signal(xl_sem, inc=1, device_id=other_xl, device_id_type=MESH)
+            for dev in others:
+                pl.semaphore_signal(plane_sem, inc=1, device_id=dev, device_id_type=MESH)
     arrived(X_UP, X_DOWN)
     rowset = pl.ds(CUT, 128 - CUT)
     part[1, rowset] += recv[FROM_YM_O, rowset]
@@ -141,11 +147,15 @@
     start(S_UP[1], S_DOWN[1])
 
     pl.semaphore_wait(z_sem, 4)
-    pl.semaphore_wait(xl_sem, 1)
+    pl.semaphore_wait(plane_sem, 3)
 
     @pl.when(y == zrow)
     def _():
         for t in range(NT):
+
+            pl.semaphore_signal(
+                line_sem, inc=1, device_id=device(xh, z, 1 - c, t // 4, t % 4), device_id_type=MESH
+            )
 
             @pl.when((xl != xh) | (me != t))
             def _():
@@ -162,42 +172,44 @@
     lane = lax.broadcasted_iota(jnp.int32, (32, 128), 1)
     fbuf[...] = jnp.where(lane < 64, gram[:32], gram[32:]).reshape(2, 2, 8, 128)
 
-    e_copy = pltpu.make_async_remote_copy(
-        src_ref=fbuf.at[1 - c], dst_ref=ebuf.at[:, c], send_sem=e_send, recv_sem=e_recv,
-        device_id=device(xl, z, 1 - c, xh, y), device_id_type=MESH,
-    )
-    e_copy.start()
-    ebuf[:, c] = fbuf[c]
-    e_copy.wait_recv()
-
-    def col_copy(to_z, to_xl):
-        return pltpu.make_async_remote_copy(
-            src_ref=ebuf.at[to_xl], dst_ref=cols.at[zpar, me],
+    def col_copy(to_z, to_xl, to_c):
+        return pltpu.make_async_remote_copy(
+            src_ref=fbuf.at[to_xl, to_c], dst_ref=cols.at[zpar, me, c],
             send_sem=col_send, recv_sem=col_recv.at[zpar],
-            device_id=device(to_xl, to_z, c, xl, zrow), device_id_type=MESH,
-        )
-
-    def row_copy(off, to_xl):
-        return pltpu.make_async_remote_copy(
-            src_ref=ebuf.at[to_xl], dst_ref=rows.at[xl, me],
+            device_id=device(to_xl, to_z, to_c, xl, zrow), device_id_type=MESH,
+        )
+
+    def row_copy(off, to_xl, to_c):
+        return pltpu.make_async_remote_copy(
+            src_ref=fbuf.at[to_xl, to_c], dst_ref=rows.at[xl, me, c],
             send_sem=row_send, recv_sem=row_recv,
-            device_id=device(to_xl, z, c, *peer(off)), device_id_type=MESH,
+            device_id=device(to_xl, z, to_c, *peer(off)), device_id_type=MESH,
         )
 
     own_line = ((xh == xl) & (y == zrow)).astype(jnp.int32)
-    pl.semaphore_wait(line_sem, 2 - own_line)
+    pl.semaphore_wait(line_sem, 4 - own_line)
     for i in range(NZ - 1):
         to_z = jnp.where(i < z, i, i + 1)
         for to_xl in (1 - xl, xl):
-            col_copy(to_z, to_xl).start()
-    for off in range(NT - 1, 0, -1):
-        row_copy(off, xl).start()
+            for to_c in (c, 1 - c):
+                col_copy(to_z, to_xl, to_c).start()
     for off in range(NT - 1, -1, -1):
-        row_copy(off, 1 - xl).start()
-    rows[xl, me] = ebuf[xl]
-
-    row_bytes = rows.reshape(32, 8, 128).at[pl.ds(0, 30)]
+        for to_xl in (1 - xl, xl):
+            for to_c in (1 - c, c):
+                if off or to_xl is not xl or to_c is not c:
+                    row_copy(off, to_xl, to_c).start()
+    rows[xl, me, c] = fbuf[xl, c]
+
+    row_bytes = rows.reshape(32, 8, 128).at[pl.ds(0, 31)]
     pltpu.make_async_copy(row_bytes, row_bytes, row_recv).wait()
+    def wide(ref):
+        return jnp.concatenate(
+            [jnp.concatenate([ref[a, :, cc, r, :] for a in range(2) for cc in range(2)], axis=0) for r in range(8)],
+            axis=1,
+        )
+
+    row_high, row_low = split(wide(rows))
+    row_split = jnp.concatenate([row_high, row_high, row_low], axis=1)
     for par in range(2):
 
         @pl.when(2 * y + par != z)
@@ -208,11 +220,8 @@
         def _():
             cols[par] = rows[xh]
 
-    acc = jnp.zeros((32, 32), jnp.float32)
-    for r in range(8):
-        col_r = jnp.concatenate([cols[par, :, cc, r, :] for par in range(2) for cc in range(2)], axis=0)
-        row_r = jnp.concatenate([rows[a, :, cc, r, :] for a in range(2) for cc in range(2)], axis=0)
-        acc = acc + contract_last(row_r, col_r, HIGHEST)
+    col_high, col_low = split(wide(cols))
+    acc = contract_last(row_split, jnp.concatenate([col_high, col_low, col_high], axis=1))
     tiles[:, :, pl.ds(0, 32)] = acc.reshape(NQ, 8, 32)
 
     def t_copy(j):
@@ -231,7 +240,6 @@
 
     for msg in MESSAGES:
         rs_copy(msg).wait_send()
-    e_copy.wait_send()
     for j in range(1, NQ):
         t_copy(j).wait_send()
     pltpu.make_async_copy(row_bytes, row_bytes, row_send).wait()
@@ -257,14 +265,12 @@
             vmem((NT, 128, length), f32),
             vmem((7, 128, length), f32),
             vmem((2, 2, 8, 128), f32),
-            vmem((2, 2, 8, 128), f32),
             vmem((2, NT, 2, 8, 128), f32),
             vmem((2, NT, 2, 8, 128), f32),
             vmem((NQ, 8, 128), f32),
             vmem((NQ, 8, 128), f32),
             dma((NT,)), dma((NT,)), dma((2,)),
             dma((len(MESSAGES),)), dma((len(MESSAGES),)),
-            dma, dma,
             dma, dma,
             dma, dma((2,)),
             dma((NQ,)), dma((NQ,)),

time: 31.1 us -> 30.6 us (0.984)
  Pallas kernels: 30.3 us -> 29.9 us
    pallas_call x1, Pallas kernels: 30.3 us -> 29.9 us  [per_device(): pl.pallas_call(kernel, out_shape=jax.ShapeDtypeStruct((8, 32), f32), in_s...]
where the time goes in v6:
time: 30.6 us; the launch traced here: 30.5 us
  Pallas kernels  29.9 us (98%)
  local copies, waits for them, and re-layouts  0.6 us (2%)
    pallas_call x1, Pallas kernels, per_device(): pl.pallas_call(kernel, out_shape=jax.ShapeDtypeStruct((8, 32), f32), in_s...  29.9 us

profile of v6, /device:TPU:18, one launch (start us, length us, event | category | flops | bytes accessed | tf_op | source)
XLA Modules:
  0.0 30.5 jit_solution(1611184905186327684)
XLA Ops:
  0.0 29.9 %shard_map.46 = f32[8,32]{1,0:T(8,128)S(1)} custom-call(bf16[8,256,1792]{2,1,0:T(8,128)(2,1)} %h_hbm.1, bf16[8,256,512]{2,1,0:T(8,128)(2,1)} %o_hbm.1, bf16[64,1792]{1,0:T(8,128)(2,1)} %pin_hbm.1, bf16[64,512]{1,0:T(8,128)(2,1)} %pout_hbm.1), custom_call_target="tpu_custom_call" | custom-call | flops 700000000 | bytes 10000000 | tf_op jit(solution)/shard_map/pallas_call | solution.py:255
  29.9 0.6 %copy.6 = f32[8,32]{1,0:T(8,128)} copy(f32[8,32]{1,0:T(8,128)S(1)} %shard_map.46) | data formatting | bytes 2048

commit v7 on v6

--- a/solution.py
+++ b/solution.py
@@ -16,14 +16,15 @@
 DEPTH = 3
 FROM_X, FROM_YM_O, FROM_YP_O, FROM_YM, FROM_YP, FROM_Y2, FROM_X_SUM = range(7)
 CUT = 112
-X_FIRST = ((6, 0, 64, FROM_X, 4), (6, 64, 64, FROM_X, 4))
+X_FIRST = ((6, 64, 64, FROM_X, 4), (6, 0, 64, FROM_X, 4))
 X_UP, X_DOWN = (5, CUT, 128 - CUT, FROM_YM_O, 4), (7, CUT, 128 - CUT, FROM_YP_O, 4)
-O_UP = tuple((5, r, CUT // 2, FROM_YM_O, 1) for r in (0, CUT // 2))
-O_DOWN = tuple((7, r, CUT // 2, FROM_YP_O, 3) for r in (0, CUT // 2))
+PIECES = ((64, CUT - 64), (0, 64))
+O_UP = tuple((5, r, n, FROM_YM_O, 1) for r, n in PIECES)
+O_DOWN = tuple((7, r, n, FROM_YP_O, 3) for r, n in PIECES)
 S_UP = ((1, 0, CUT, FROM_YM, 1), (1, CUT, 128 - CUT, FROM_YM, 1))
 S_DOWN = ((3, 0, CUT, FROM_YP, 3), (3, CUT, 128 - CUT, FROM_YP, 3))
-S_ACROSS = ((2, 0, 64, FROM_Y2, 2), (2, 64, 64, FROM_Y2, 2))
-X_SUM = ((4, 0, CUT // 2, FROM_X_SUM, 4), (4, CUT // 2, CUT // 2, FROM_X_SUM, 4), (4, CUT, 128 - CUT, FROM_X_SUM, 4))
+S_ACROSS = ((2, 64, 64, FROM_Y2, 2), (2, 0, 64, FROM_Y2, 2))
+X_SUM = tuple((4, r, n, FROM_X_SUM, 4) for r, n in PIECES + ((CUT, 128 - CUT),))
 MESSAGES = X_FIRST + (X_UP, X_DOWN) + O_UP + O_DOWN + S_UP + S_DOWN + S_ACROSS + X_SUM
 
 
@@ -59,18 +60,20 @@
     win = pltpu.make_async_copy(pin_hbm, wl, wsem.at[0])
     wout = pltpu.make_async_copy(pout_hbm, wr, wsem.at[1])
 
-    def load(off):
+    def load_left(off):
         a, b = peer(off)
-        return (
-            pltpu.make_async_copy(h_hbm.at[a * 4 + b], hbuf.at[off], hsem.at[off]),
-            pltpu.make_async_copy(o_hbm.at[a * 4 + b], obuf.at[off], osem.at[off]),
-        )
-
-    win.start()
+        return pltpu.make_async_copy(h_hbm.at[a * 4 + b], hbuf.at[off], hsem.at[off])
+
+    def load_right(off):
+        a, b = peer(off)
+        return pltpu.make_async_copy(o_hbm.at[a * 4 + b], obuf.at[off], osem.at[off])
+
     wout.start()
     for off in ORDER[:DEPTH]:
-        for copy in load(off):
-            copy.start()
+        load_right(off).start()
+    win.start()
+    for off in ORDER[:DEPTH]:
+        load_left(off).start()
 
     barrier = pltpu.get_barrier_semaphore()
 
@@ -85,18 +88,22 @@
     greetings = 11
 
     tiles[...] = jnp.zeros_like(tiles)
-    win.wait()
-    wout.wait()
-
-    def project(off):
-        for copy in load(off):
-            copy.wait()
+
+    def project_left(off):
+        load_left(off).wait()
         ahead = ORDER.index(off) + DEPTH
         if ahead < NT:
-            for copy in load(ORDER[ahead]):
-                copy.start()
+            load_right(ORDER[ahead]).start()
+            load_left(ORDER[ahead]).start()
         part[off, pl.ds(0, 64)] = contract_last(wl[...], hbuf[off])
+
+    def project_right(off):
+        load_right(off).wait()
         part[off, pl.ds(64, 64)] = contract_last(wr[...], obuf[off])
+
+    def project(off):
+        project_right(off)
+        project_left(off)
 
     def rs_copy(msg):
         chunk, row, count, slot, to = msg
@@ -115,10 +122,18 @@
         for msg in messages:
             rs_copy(msg).wait_recv()
 
+    wout.wait()
     for off in (5, 7, 6):
-        project(off)
+        project_right(off)
+    win.wait()
+    project_left(5)
     pl.semaphore_wait(barrier, greetings)
-    start(O_UP[0], O_DOWN[0], X_FIRST[0], O_UP[1], O_DOWN[1], X_FIRST[1], X_UP, X_DOWN)
+    start(O_UP[0], O_DOWN[0], X_FIRST[0], X_UP, X_DOWN)
+    start(O_UP[1])
+    project_left(7)
+    start(O_DOWN[1])
+    project_left(6)
+    start(X_FIRST[1])
     for dev in near_z:
         pl.semaphore_signal(z_sem, inc=1, device_id=dev, device_id_type=MESH)
     project(1)
@@ -130,11 +145,11 @@
     project(2)
     for half in range(2):
         arrived(O_UP[half], O_DOWN[half])
-        rowset = pl.ds(CUT // 2 * half, CUT // 2)
+        rowset = pl.ds(*PIECES[half])
         part[4, rowset] += recv[FROM_YM_O, rowset] + recv[FROM_YP_O, rowset]
         start(X_SUM[half])
         arrived(X_FIRST[half])
-        rowset = pl.ds(64 * half, 64)
+        rowset = pl.ds(64 - 64 * half, 64)
         part[2, rowset] += recv[FROM_X, rowset]
         start(S_ACROSS[half])
         if half == 0:

time: 30.6 us -> 29.7 us (0.971)
  Pallas kernels: 29.9 us -> 29.1 us
    pallas_call x1, Pallas kernels: 29.9 us -> 29.1 us  [per_device(): pl.pallas_call(kernel, out_shape=jax.ShapeDtypeStruct((8, 32), f32), in_s...]
where the time goes in v7:
time: 29.7 us
  Pallas kernels  29.1 us (98%)
  local copies, waits for them, and re-layouts  0.6 us (2%)
    pallas_call x1, Pallas kernels, per_device(): pl.pallas_call(kernel, out_shape=jax.ShapeDtypeStruct((8, 32), f32), in_s...  29.1 us
    unnamed x1, local copies, waits for them, and re-layouts  0.6 us

profile of v7, /device:TPU:18, one launch (start us, length us, event | category | flops | bytes accessed | tf_op | source)
XLA Modules:
  0.0 29.7 jit_solution(9889431111335129238)
XLA Ops:
  0.0 29.1 %shard_map.46 = f32[8,32]{1,0:T(8,128)S(1)} custom-call(bf16[8,256,1792]{2,1,0:T(8,128)(2,1)} %h_hbm.1, bf16[8,256,512]{2,1,0:T(8,128)(2,1)} %o_hbm.1, bf16[64,1792]{1,0:T(8,128)(2,1)} %pin_hbm.1, bf16[64,512]{1,0:T(8,128)(2,1)} %pout_hbm.1), custom_call_target="tpu_custom_call" | custom-call | flops 700000000 | bytes 10000000 | tf_op jit(solution)/shard_map/pallas_call | solution.py:270
  29.1 0.6 %copy.6 = f32[8,32]{1,0:T(8,128)} copy(f32[8,32]{1,0:T(8,128)S(1)} %shard_map.46) | data formatting | bytes 2048

commit v8 on v7

--- a/solution.py
+++ b/solution.py
@@ -21,8 +21,8 @@
 PIECES = ((64, CUT - 64), (0, 64))
 O_UP = tuple((5, r, n, FROM_YM_O, 1) for r, n in PIECES)
 O_DOWN = tuple((7, r, n, FROM_YP_O, 3) for r, n in PIECES)
-S_UP = ((1, 0, CUT, FROM_YM, 1), (1, CUT, 128 - CUT, FROM_YM, 1))
-S_DOWN = ((3, 0, CUT, FROM_YP, 3), (3, CUT, 128 - CUT, FROM_YP, 3))
+S_UP = tuple((1, r, n, FROM_YM, 1) for r, n in PIECES + ((CUT, 128 - CUT),))
+S_DOWN = tuple((3, r, n, FROM_YP, 3) for r, n in PIECES + ((CUT, 128 - CUT),))
 S_ACROSS = ((2, 64, 64, FROM_Y2, 2), (2, 0, 64, FROM_Y2, 2))
 X_SUM = tuple((4, r, n, FROM_X_SUM, 4) for r, n in PIECES + ((CUT, 128 - CUT),))
 MESSAGES = X_FIRST + (X_UP, X_DOWN) + O_UP + O_DOWN + S_UP + S_DOWN + S_ACROSS + X_SUM
@@ -136,10 +136,14 @@
     start(X_FIRST[1])
     for dev in near_z:
         pl.semaphore_signal(z_sem, inc=1, device_id=dev, device_id_type=MESH)
-    project(1)
+    project_right(1)
     start(S_UP[0])
-    project(3)
+    project_right(3)
     start(S_DOWN[0])
+    project_left(1)
+    start(S_UP[1])
+    project_left(3)
+    start(S_DOWN[1])
     project(4)
     start(X_SUM[2])
     project(2)
@@ -159,7 +163,7 @@
     rowset = pl.ds(CUT, 128 - CUT)
     part[1, rowset] += recv[FROM_YM_O, rowset]
     part[3, rowset] += recv[FROM_YP_O, rowset]
-    start(S_UP[1], S_DOWN[1])
+    start(S_UP[2], S_DOWN[2])
 
     pl.semaphore_wait(z_sem, 4)
     pl.semaphore_wait(plane_sem, 3)

time: 29.7 us -> 29.6 us (level)
  no operation moved by 1% of the time
where the time goes in v8:
time: 29.6 us
  Pallas kernels  28.9 us (98%)
  local copies, waits for them, and re-layouts  0.6 us (2%)
    pallas_call x1, Pallas kernels, per_device(): pl.pallas_call(kernel, out_shape=jax.ShapeDtypeStruct((8, 32), f32), in_s...  28.9 us
    unnamed x1, local copies, waits for them, and re-layouts  0.6 us

profile of v8, /device:TPU:18, one launch (start us, length us, event | category | flops | bytes accessed | tf_op | source)
XLA Modules:
  0.0 29.6 jit_solution(16416101387673249620)
XLA Ops:
  0.0 28.9 %shard_map.46 = f32[8,32]{1,0:T(8,128)S(1)} custom-call(bf16[8,256,1792]{2,1,0:T(8,128)(2,1)} %h_hbm.1, bf16[8,256,512]{2,1,0:T(8,128)(2,1)} %o_hbm.1, bf16[64,1792]{1,0:T(8,128)(2,1)} %pin_hbm.1, bf16[64,512]{1,0:T(8,128)(2,1)} %pout_hbm.1), custom_call_target="tpu_custom_call" | custom-call | flops 700000000 | bytes 10000000 | tf_op jit(solution)/shard_map/pallas_call | solution.py:274
  29.0 0.6 %copy.6 = f32[8,32]{1,0:T(8,128)} copy(f32[8,32]{1,0:T(8,128)S(1)} %shard_map.46) | data formatting | bytes 2048

commit v9 on v8

--- a/solution.py
+++ b/solution.py
@@ -148,14 +148,14 @@
     start(X_SUM[2])
     project(2)
     for half in range(2):
+        arrived(X_FIRST[half])
+        rowset = pl.ds(64 - 64 * half, 64)
+        part[2, rowset] += recv[FROM_X, rowset]
+        start(S_ACROSS[half])
         arrived(O_UP[half], O_DOWN[half])
         rowset = pl.ds(*PIECES[half])
         part[4, rowset] += recv[FROM_YM_O, rowset] + recv[FROM_YP_O, rowset]
         start(X_SUM[half])
-        arrived(X_FIRST[half])
-        rowset = pl.ds(64 - 64 * half, 64)
-        part[2, rowset] += recv[FROM_X, rowset]
-        start(S_ACROSS[half])
         if half == 0:
             for dev in others:
                 pl.semaphore_signal(plane_sem, inc=1, device_id=dev, device_id_type=MESH)

time: 29.6 us -> 29.6 us (level)
  no operation moved by 1% of the time
where the time goes in v9:
time: 29.6 us
  Pallas kernels  28.9 us (98%)
  local copies, waits for them, and re-layouts  0.6 us (2%)
    pallas_call x1, Pallas kernels, per_device(): pl.pallas_call(kernel, out_shape=jax.ShapeDtypeStruct((8, 32), f32), in_s...  28.9 us
    unnamed x1, local copies, waits for them, and re-layouts  0.6 us

profile of v9, /device:TPU:18, one launch (start us, length us, event | category | flops | bytes accessed | tf_op | source)
XLA Modules:
  0.0 29.6 jit_solution(951960996734529744)
XLA Ops:
  0.0 28.9 %shard_map.46 = f32[8,32]{1,0:T(8,128)S(1)} custom-call(bf16[8,256,1792]{2,1,0:T(8,128)(2,1)} %h_hbm.1, bf16[8,256,512]{2,1,0:T(8,128)(2,1)} %o_hbm.1, bf16[64,1792]{1,0:T(8,128)(2,1)} %pin_hbm.1, bf16[64,512]{1,0:T(8,128)(2,1)} %pout_hbm.1), custom_call_target="tpu_custom_call" | custom-call | flops 700000000 | bytes 10000000 | tf_op jit(solution)/shard_map/pallas_call | solution.py:274
  29.0 0.6 %copy.6 = f32[8,32]{1,0:T(8,128)} copy(f32[8,32]{1,0:T(8,128)S(1)} %shard_map.46) | data formatting | bytes 2048
